TPU v7x, 128 devices: a whole 4x4x4 slice. The times are simulated.
128 devices in a mesh: grp: 8 (over x, core), mem: 16 (over z, y).
Axes of the slice: x: 4, y: 4, z: 4, core: 2. Of those that a mesh axis runs over, the one named last changes fastest.
Arguments:
- embeddings: bfloat16 [131072, 768], P(('grp', 'mem'))
- cluster: int32 [131072], P(('grp', 'mem')), may hold values from -1 to 15, as said below
- rank: int32 [131072], P(('grp', 'mem')), may hold values from -1 to 8191, as said below
Outputs:
- best_match: float32 [131072], P(('grp', 'mem'))
Inputs may be any that keep to these rules, and one draw needn't show every extreme that they name: cluster is -1 exactly where rank is -1. Ranks are distinct within a cluster; among the rows of one device, at most 4 have the same cluster // 2 and the same rank // 256, and every device reaches 4 for some such pair.
All inputs are finite; a program needn't handle non-finite values.
Results may differ from a plain program's by a relative error of at most 0.0004.
Values may be sent and summed in bfloat16 or wider, within the bound.
A program may use at most 128 MiB of HBM per device.

v0:
```python
import jax
import jax.numpy as jnp
from jax import lax
from jax.sharding import PartitionSpec as P

CLUS_GRP = 2


def unit_rows(embeddings):
    wide = embeddings.astype(jnp.float32)
    total = jnp.sum(wide * wide, axis=1, keepdims=True)
    return (wide * lax.rsqrt(total + 1e-06)).astype(jnp.bfloat16)


def half_of(device, which):
    return 2 * device + which


def owner_of(half_id):
    return (half_id // 2, half_id % 2)


def on_device(embeddings, cluster, rank):
    rows_dev, width = embeddings.shape
    groups = lax.axis_size("grp")
    members = lax.axis_size("mem")
    devices = groups * members
    clus_grp = CLUS_GRP
    slot_dev = rows_dev // clus_grp
    half = slot_dev // 2
    quota = rows_dev // devices
    unit = unit_rows(embeddings)
    alive = cluster >= 0
    safe_cluster = jnp.maximum(cluster, 0)
    safe_rank = jnp.maximum(rank, 0)
    member_id, which_half = owner_of(safe_rank // half)
    target = safe_cluster // clus_grp * members + member_id
    slot = safe_cluster % clus_grp * slot_dev + which_half * half + safe_rank % half
    hits = (target[:, None] == jnp.arange(devices, dtype=jnp.int32)[None, :]) & alive[:, None]
    hit_count = hits.astype(jnp.int32)
    before = jnp.cumsum(hit_count, axis=0) - hit_count
    position = jnp.sum(jnp.where(hits, before, 0), axis=1)
    send_at = jnp.where(alive, target * quota + position, devices * quota)
    outgoing = jnp.zeros((devices * quota + 1, width), jnp.bfloat16).at[send_at].set(unit)[:-1]
    labels = (
        jnp.full((devices * quota + 1,), -1, jnp.int32)
        .at[send_at]
        .set(jnp.where(alive, slot, -1))[:-1]
    )
    arrived, arrived_slot = (
        lax.all_to_all(outgoing, ("grp", "mem"), split_axis=0, concat_axis=0, tiled=True),
        lax.all_to_all(labels, ("grp", "mem"), split_axis=0, concat_axis=0, tiled=True),
    )
    filled = arrived_slot >= 0
    place_at = jnp.where(filled, arrived_slot, clus_grp * slot_dev)
    grid = (
        jnp.zeros((clus_grp * slot_dev + 1, width), jnp.bfloat16)
        .at[place_at]
        .set(arrived)[:-1]
        .reshape(clus_grp, slot_dev, width)
    )
    present = (
        jnp.zeros((clus_grp * slot_dev + 1,), jnp.bfloat16)
        .at[place_at]
        .set(jnp.ones_like(arrived_slot, jnp.bfloat16))[:-1]
        .reshape(clus_grp, slot_dev)
    )
    me = lax.axis_index("mem")
    my_halves = (half_of(me, 0), half_of(me, 1))
    offsets = jnp.arange(half, dtype=jnp.int32)

    def column_ranks(spots):
        return half_of(spots // slot_dev, spots % slot_dev // half) * half + spots % half

    def compare(rows, row_half, cols, col_rank, col_live):
        sims = jnp.einsum("crd,cjd->crj", rows, cols, preferred_element_type=jnp.float32)
        row_rank = row_half * half + offsets
        keep = (col_rank[None, None, :] < row_rank[None, :, None]) & (col_live[:, None, :] > 0)
        return jnp.max(jnp.where(keep, sims, jnp.float32(-1.0)), axis=2)

    initial = jnp.full((clus_grp, slot_dev), -1.0, jnp.float32)
    cols_all = lax.all_gather(grid, "mem", axis=1, tiled=True)
    live_all = lax.all_gather(present, "mem", axis=1, tiled=True)
    span = cols_all.shape[1]

    def one_tile(step, acc):
        anchor = step * half
        cols = lax.dynamic_slice_in_dim(cols_all, step * half, half, 1)
        live = lax.dynamic_slice_in_dim(live_all, step * half, half, 1)
        col_rank = column_ranks(anchor + offsets)
        results = []
        for which in range(2):
            rows = grid[:, which * half : (which + 1) * half]
            row_half = my_halves[which]
            fresh = lax.cond(
                jnp.min(col_rank) < (row_half + 1) * half,
                lambda operands: compare(*operands),
                lambda operands: jnp.full((clus_grp, half), -1.0, jnp.float32),
                (rows, row_half, cols, col_rank, live),
            )
            results.append(fresh)
        return jnp.maximum(acc, jnp.concatenate(results, axis=1))

    best = lax.fori_loop(0, span // half, one_tile, initial)
    reply = jnp.where(
        filled, best.reshape(-1)[jnp.where(filled, arrived_slot, 0)], jnp.float32(-1.0)
    )
    back = lax.all_to_all(reply, ("grp", "mem"), split_axis=0, concat_axis=0, tiled=True)
    return jnp.where(alive, back[jnp.minimum(send_at, devices * quota - 1)], jnp.float32(-1.0))


def solution(mesh):
    in_specs = (P(("grp", "mem"), None), P(("grp", "mem")), P(("grp", "mem")))
    out_specs = P(("grp", "mem"))
    return jax.shard_map(
        on_device, mesh=mesh, in_specs=in_specs, out_specs=out_specs, check_vma=False
    )
```

profile of v0, /device:TPU:1, one launch (start us, length us, event | category | flops | bytes accessed | tf_op | source)
XLA Modules:
  0.0 398.4 jit_solution(18385969982864803251)
XLA Ops:
  8.6 4.3 %scatter_custom_fusion = s32[1025]{0:T(1024)S(1)} fusion(s32[1024]{0:T(1024)S(1)} %get-tuple-element.412, s32[1024]{0:T(1024)S(1)} %get-tuple-element.407, s32[]{:T(128)} %constant.264.clone.1), kind=kCustom, calls=%fused_computation.88 | custom fusion | bytes 4104 | tf_op jit(solution)/shard_map/scatter | solution.py:48
  13.6 11.5 %all-to-all-start = ((s32[128,8,1]{1,2,0:T(1,128)}), s32[128,8,1]{1,2,0:T(1,128)S(1)}, u32[]{:S(2)}, u32[]{:S(2)}) async-start(s32[128,8,1]{1,2,0:T(1,128)} %bitcast.5), calls=%async_computation | async-start | bytes 131072 | tf_op jit(solution)/shard_map/all_to_all | solution.py:52
  25.5 6.0 %scatter_custom_fusion.1 = bf16[1025,768]{1,0:T(8,128)(2,1)S(1)} fusion(s32[1024]{0:T(1024)S(1)} %get-tuple-element.412, bf16[1024,768]{1,0:T(8,128)(2,1)S(1)} %copy-done.1, f32[1024]{0:T(1024)S(1)} %add_rsqrt_fusion, bf16[]{:T(256)} %constant.275.clone.1), kind=kCustom, calls=%fused_computation.39 | custom fusion | flops 2359296 | bytes 3151362 | tf_op jit(solution)/shard_map/scatter | solution.py:44
  31.5 1.3 slice_bitcast_fusion
  32.8 2.1 all-to-all-done
  34.9 7.7 %all-to-all-start.1 = ((bf16[128,8,768]{2,1,0:T(8,128)(2,1)}), bf16[128,8,768]{2,1,0:T(8,128)(2,1)S(1)}, u32[]{:S(2)}, u32[]{:S(2)}) async-start(bf16[128,8,768]{2,1,0:T(8,128)(2,1)} %slice_bitcast_fusion), calls=%async_computation.1 | async-start | bytes 3145728 | tf_op jit(solution)/shard_map/all_to_all | solution.py:51
  44.1 22.6 %all-to-all-done.1 = bf16[128,8,768]{2,1,0:T(8,128)(2,1)S(1)} async-done(((bf16[128,8,768]{2,1,0:T(8,128)(2,1)}), bf16[128,8,768]{2,1,0:T(8,128)(2,1)S(1)}, u32[]{:S(2)}, u32[]{:S(2)}) %all-to-all-start.1) | async-done | bytes 1572896 | tf_op jit(solution)/shard_map/all_to_all | solution.py:51
  66.7 5.8 %scatter_custom_fusion.2 = bf16[1025,768]{1,0:T(8,128)(2,1)S(1)} fusion(s32[1024]{0:T(1024)S(1)} %bitcast.38, bf16[128,8,768]{2,1,0:T(8,128)(2,1)S(1)} %all-to-all-done.1, bf16[]{:T(256)} %constant.275.clone.1), kind=kCustom, calls=%fused_computation.41 | custom fusion | bytes 3147266 | tf_op jit(solution)/shard_map/scatter | solution.py:59
  72.5 1.3 slice.50
  73.9 7.6 %scatter_custom_fusion.3 = bf16[1025]{0:T(1024)(128)(2,1)S(1)} fusion(s32[1024]{0:T(1024)S(1)} %bitcast.39, bf16[1024]{0:T(1024)(128)(2,1)S(1)} %broadcast.285, bf16[]{:T(256)} %constant.275.clone.1), kind=kCustom, calls=%fused_computation.98 | custom fusion | bytes 2052 | tf_op jit(solution)/shard_map/scatter | solution.py:65
  81.5 19.3 %all_gather.7 = bf16[2,8192]{1,0:T(2,128)(2,1)S(1)} all-gather(bf16[2,512]{1,0:T(2,128)(2,1)S(1)} %reshape.163), channel_id=1, replica_groups=mesh['grp'=8,'mem'=16] {'mem'}, dimensions={1}, use_global_device_ids=true | all-gather | bytes 34816 | tf_op jit(solution)/shard_map/all_gather | solution.py:83
  100.8 123.9 %all-gather.2.cloned.1.call-done = bf16[2,8192,768]{2,1,0:T(8,128)(2,1)} async-done(((bf16[2,512,768]{2,1,0:T(8,128)(2,1)}), bf16[2,8192,768]{2,1,0:T(8,128)(2,1)}) %all-gather.2.cloned.1.call-update) | async-done | bytes 25165840 | tf_op jit(solution)/shard_map/all_gather | solution.py:82
  224.7 105.3 %while.18 = (s32[]{:T(128)}, f32[2,512]{1,0:T(2,128)S(1)}, s32[]{:T(128)}, bf16[2,8192,768]{2,1,0:T(8,128)(2,1)}, bf16[2,8192]{1,0:T(2,128)(2,1)S(1)}, /*index=5...) while((s32[]{:T(128)}, f32[2,512]{1,0:T(2,128)S(1)}, ...), condition=%wide.region_16.17_spmd.clone.clone, body=%wide.region_8.16_spmd.clone.clone.sunk | while | flops 403586560 | bytes 5014897 | solution.py:104
  229.1 1.2 constant_dynamic-slice_fusion.5
  232.9 1.2 constant_dynamic-slice_fusion.5
  242.6 1.2 constant_dynamic-slice_fusion.5
  252.3 1.2 constant_dynamic-slice_fusion.5
  284.7 1.2 constant_dynamic-slice_fusion.5
  294.4 1.2 constant_dynamic-slice_fusion.5
  304.1 1.2 constant_dynamic-slice_fusion.5
  313.9 1.2 constant_dynamic-slice_fusion.5
  330.0 4.5 %gather_fusion = f32[1024]{0:T(1024)S(1)} fusion(f32[1024]{0:T(1024)S(1)} %bitcast.29, s32[1024]{0:T(1024)S(1)} %broadcast_clamp_fusion), kind=kCustom, calls=%fused_computation | custom fusion | bytes 12288 | tf_op jit(solution)/shard_map/gather | solution.py:106
  334.7 50.3 %all_to_all.33 = f32[128,8,1]{1,2,0:T(1,128)S(1)} all-to-all(f32[128,8,1]{1,2,0:T(1,128)S(1)} %bitcast.33), channel_id=1, replica_groups=mesh['grp'=8,'mem'=16] {'grp','mem'}, dimensions={0} | all-to-all | bytes 8192 | tf_op jit(solution)/shard_map/all_to_all | solution.py:108
  386.4 4.5 %gather_fusion.1 = f32[1024]{0:T(1024)S(1)} fusion(f32[1024]{0:T(1024)S(1)} %all_to_all.29, s32[1024]{0:T(1024)S(1)} %get-tuple-element.411), kind=kCustom, calls=%fused_computation.1 | custom fusion | bytes 12288 | tf_op jit(solution)/shard_map/gather | solution.py:109
  (326 shorter events, 62.3 us)
Async XLA Ops:
  7.8 17.3 %copy-start.1 = (bf16[1024,768]{1,0:T(8,128)(2,1)S(1)}, bf16[1024,768]{1,0:T(8,128)(2,1)}, u32[]{:S(2)}) copy-start(bf16[1024,768]{1,0:T(8,128)(2,1)} %param.9) | copy-start | bytes 4718596
  13.6 21.3 %all-to-all-start = ((s32[128,8,1]{1,2,0:T(1,128)}), s32[128,8,1]{1,2,0:T(1,128)S(1)}, u32[]{:S(2)}, u32[]{:S(2)}) async-start(s32[128,8,1]{1,2,0:T(1,128)} %bitcast.5), calls=%async_computation | async-start | bytes 131072 | tf_op jit(solution)/shard_map/all_to_all | solution.py:52
  34.9 31.8 %all-to-all-start.1 = ((bf16[128,8,768]{2,1,0:T(8,128)(2,1)}), bf16[128,8,768]{2,1,0:T(8,128)(2,1)S(1)}, u32[]{:S(2)}, u32[]{:S(2)}) async-start(bf16[128,8,768]{2,1,0:T(8,128)(2,1)} %slice_bitcast_fusion), calls=%async_computation.1 | async-start | bytes 3145728 | tf_op jit(solution)/shard_map/all_to_all | solution.py:51
  42.6 182.1 %all-gather.2.cloned.1.call-start = ((), (), s32[]{:S(2)}) async-start(), calls=%async_computation.3 | async-start | bytes 26738688 | tf_op jit(solution)/shard_map/all_gather | solution.py:82
  73.8 150.9 %copy-start = (bf16[1024,768]{1,0:T(8,128)(2,1)S(1)}, bf16[1024,768]{1,0:T(8,128)(2,1)}, u32[]{:S(2)}) copy-start(bf16[1024,768]{1,0:T(8,128)(2,1)} %slice.50) | copy-start | bytes 4718596
Sparse Core Ops, SparseCore 0:
  73.9 150.7 all-gather.1
where the time goes:
time: 401 us; the launch traced here: 398 us
  waiting for transfers between devices  149 us (37%)
  local copies, waits for them, and re-layouts  70.5 us (18%)
  blocking collectives  69.6 us (17%)
  loops' own time  43.2 us (11%)
  other arithmetic  32.3 us (8%)
  starting transfers between devices  19.2 us (5%)
  between operations  13.6 us (3%)
    all_gather x1, waiting for transfers between devices, on_device(): cols_all = lax.all_gather(grid, 'mem', axis=1, tiled=True)  124 us
    all_to_all x1, blocking collectives, on_device(): lax.all_to_all(reply, ('grp', 'mem'), split_axis=0, concat_axis=0, tiled=...  50.3 us
    another operation x1, loops' own time, on_device(): best = lax.fori_loop(0, span // half, one_tile, initial)  41.9 us
    dynamic_slice x32, local copies, waits for them, and re-layouts, one_tile(): cols = lax.dynamic_slice_in_dim(cols_all, step * half, half, 1)  38.2 us
    all_to_all x1, waiting for transfers between devices, on_device(): lax.all_to_all(outgoing, ('grp', 'mem'), split_axis=0, concat_axis=0, til...  22.6 us
    add x32, other arithmetic, column_ranks(): half_of(spots // slot_dev, spots % slot_dev // half) * half + spots % half  21.2 us
    all_gather x1, blocking collectives, on_device(): live_all = lax.all_gather(present, 'mem', axis=1, tiled=True)  19.3 us
    all_to_all x1, starting transfers between devices, on_device(): lax.all_to_all(labels, ('grp', 'mem'), split_axis=0, concat_axis=0, tiled...  11.5 us
  transfers between devices with their start and end apart: 3, of which 3 were waited for; matrix products, arithmetic and copies ran while one was open for 4% of the time, Pallas kernels for 0%

commit v1 on v0

v1 whole, which is shorter than its diff:
```python
import functools

import jax
import jax.numpy as jnp
from jax import lax
from jax.experimental import pallas as pl
from jax.experimental.pallas import tpu as pltpu
from jax.sharding import PartitionSpec as P

MESH = pl.DeviceIdType.MESH
D = 768
WIDE = 896
ROWS = 1024
HALF = 256
DEVS = 128
BF = jnp.bfloat16
F32 = jnp.float32
I32 = jnp.int32

BLOCKS = ((0, 1), (0, 1), (0, 2), (0, 3), (1, 2), (1, 3), (2, 3), (2, 3))
SHARERS = ((0, 1, 2, 3), (0, 1, 4, 5), (2, 4, 6, 7), (3, 5, 6, 7))
PLACE = ((3, 1, 1), (3, 0, 1), (0, 1, 1), (2, 0, 1), (0, 1, 0), (2, 0, 0), (1, 1, 0), (1, 0, 0))


def pick(index, table):
    out = jnp.int32(table[0])
    for at, value in enumerate(table):
        if at:
            out = jnp.where(index == at, jnp.int32(value), out)
    return out


def pick_vec(index, table):
    out = jnp.full_like(index, table[0])
    for at, value in enumerate(table):
        if at:
            out = jnp.where(index == at, jnp.int32(value), out)
    return out


def device_of(g, k, core):
    x = pick(k, [p[0] for p in PLACE])
    y = lax.rem(pick(k, [p[1] for p in PLACE]) + lax.div(g, 2), 4)
    z = lax.rem(pick(k, [p[2] for p in PLACE]) + lax.rem(lax.div(g, 2), 2) + 2 * lax.rem(g, 2), 4)
    return 2 * x + core, 4 * z + y


def my_place():
    grp, mem = lax.axis_index("grp"), lax.axis_index("mem")
    x, core = lax.div(grp, 2), lax.rem(grp, 2)
    z, y = lax.div(mem, 4), lax.rem(mem, 4)
    odd = lax.rem(y + z, 2)
    k = pick(2 * x + odd, [2, 4, 7, 6, 5, 3, 0, 1])
    gy = lax.rem(y - pick(k, [p[1] for p in PLACE]) + 4, 4)
    gz = lax.rem(z - pick(k, [p[2] for p in PLACE]) - lax.rem(gy, 2) + 8, 4)
    return grp, mem, 2 * gy + lax.div(gz, 2), k, core


FLAT_SHARERS = [k for row in SHARERS for k in row]
FLAT_POS = [BLOCKS[k].index(b) for b in range(4) for k in SHARERS[b]]
FLAT_BLOCKS = [b for pair in BLOCKS for b in pair]
FLAT_TURN = [SHARERS[BLOCKS[k][p]].index(k) for k in range(8) for p in range(2)]

NT = (((1,), (1,)), ((), ()))
NN = (((1,), (0,)), ((), ()))


def mm(a, b, dims=NN):
    return lax.dot_general(a, b, dims, preferred_element_type=F32)


def kernel(emb_ref, clu_ref, rank_ref, out_ref, unit, packed, arrived, split, held, acc, pbest,
           rbest, rep, back, send0, recv0, send1, recv1, send2, recv2, send3, recv3):
    grp, mem, g, k, core = my_place()
    me = grp * 16 + mem

    barrier = pltpu.get_barrier_semaphore()

    @pl.loop(1, DEVS)
    def _(j):
        d = lax.rem(me + j, DEVS)
        pl.semaphore_signal(barrier, inc=1, device_id=(lax.div(d, 16), lax.rem(d, 16)), device_id_type=MESH)

    @pl.loop(0, 4)
    def _(i):
        rows = pl.ds(pl.multiple_of(i * 256, 256), 256)
        wide = emb_ref[rows, :].astype(F32)
        total = jnp.sum(wide * wide, axis=1, keepdims=True)
        unit[rows, :] = (wide * lax.rsqrt(total + 1e-06)).astype(BF)

    clu, rank = clu_ref[...], rank_ref[...]
    alive = clu >= 0
    vg = clu >> 1
    vh = rank >> 8
    share = ((vh >> 3) << 2) + ((vh & 7) >> 1)
    vk = pick_vec(share, FLAT_SHARERS)
    vp = pick_vec(share, FLAT_POS)
    vx = pick_vec(vk, [p[0] for p in PLACE])
    vy = (pick_vec(vk, [p[1] for p in PLACE]) + (vg >> 1)) & 3
    vz = (pick_vec(vk, [p[2] for p in PLACE]) + ((vg >> 1) & 1) + 2 * (vg & 1)) & 3
    vdev = (2 * vx + (vh & 1)) * 16 + 4 * vz + vy
    bucket = jnp.where(alive, 2 * vdev + vp, -1)
    low = lax.broadcasted_iota(I32, (128, 256), 0)
    col = lax.broadcasted_iota(I32, (128, 256), 1)
    tri = jnp.where((low < col) | (col >= 128), 1.0, 0.0).astype(BF)
    carry = jnp.zeros((256, 128), F32)
    bid = lax.broadcasted_iota(I32, (256, 128), 0)
    spots = []
    for i in range(8):
        hit = bid == bucket[:, i * 128 : (i + 1) * 128]
        counts = mm(jnp.where(hit, 1.0, 0.0).astype(BF), tri)
        spots.append(jnp.sum(jnp.where(hit, counts[:, :128] + carry, 0.0), axis=0, keepdims=True))
        carry = carry + counts[:, 128:]
    spot = jnp.concatenate(spots, axis=1).astype(I32)
    send_at = jnp.where(alive, bucket * 4 + spot, -1)

    kind = lax.broadcasted_iota(I32, (128, ROWS), 0)
    labels = jnp.where(
        kind == 0, (rank & 255).astype(F32), jnp.where(kind == 1, (clu & 1).astype(F32), jnp.where(kind == 2, 1.0, 0.0))
    ).astype(BF)

    @pl.loop(0, 4)
    def _(i):
        line = lax.broadcasted_iota(I32, (256, ROWS), 0) + i * 256
        where_to = jnp.where(line == send_at, 1.0, 0.0).astype(BF)
        devs = pl.ds(pl.multiple_of(i * 32, 32), 32)
        packed[devs, :, 0:D] = mm(where_to, unit[...]).reshape(32, 8, D).astype(BF)
        packed[devs, :, D:WIDE] = mm(where_to, labels, NT).reshape(32, 8, 128).astype(BF)

    pl.semaphore_wait(barrier, DEVS - 1)

    pltpu.make_async_copy(packed.at[me], arrived.at[me], recv0).start()

    @pl.loop(1, DEVS)
    def _(j):
        d = lax.rem(me + 37 * j, DEVS)
        pltpu.make_async_remote_copy(
            src_ref=packed.at[d], dst_ref=arrived.at[me], send_sem=send0, recv_sem=recv0,
            device_id=(lax.div(d, 16), lax.rem(d, 16)), device_id_type=MESH,
        ).start()

    acc[...] = jnp.full(acc.shape, -1.0, F32)
    pltpu.make_async_copy(arrived, arrived, recv0).wait()

    got = arrived[...].reshape(ROWS, WIDE)
    got_labels = got[:, D:WIDE]
    lane = lax.broadcasted_iota(I32, (8, 128), 1)
    weigh = jnp.where(lane == 0, 1.0, jnp.where(lane == 1, 256.0, jnp.where(lane == 2, 2048.0, 0.0))).astype(BF)
    slot_row = mm(weigh, got_labels, NT)[0:1, :].astype(I32)
    arr_i = lax.broadcasted_iota(I32, (1, ROWS), 1)
    slot_row = jnp.where(slot_row >= 2048, slot_row - 2048 + ((arr_i >> 2) & 1) * 512, -1)
    first = lax.broadcasted_iota(I32, (256, 128), 1) == 0

    for b in range(2):
        block = pick(2 * k + b, FLAT_BLOCKS)
        turn = pick(2 * k + b, FLAT_TURN)
        for c in range(2):
            n = 2 * b + c
            line = lax.broadcasted_iota(I32, (256, ROWS), 0) + n * 256
            where_to = jnp.where(line == slot_row, 1.0, 0.0).astype(BF)
            rows = mm(where_to, got)
            here = rows[:, D + 2 : D + 3]
            split[n, :, 0:128] = jnp.where(first & (here < 0.5), 256.0, rows[:, 0:128]).astype(BF)
            split[n, :, 128:D] = rows[:, 128:D].astype(BF)
            for t in range(4):
                other = pick(4 * block + t, FLAT_SHARERS)
                pos = pick(4 * block + t, FLAT_POS)
                mine = (other == k) & (core == c)

                @pl.when(mine)
                def _():
                    pltpu.make_async_copy(split.at[n], held.at[pos, 2 * turn + core], recv1.at[pos, 2 * turn + core]).start()

                @pl.when(jnp.logical_not(mine))
                def _():
                    pltpu.make_async_remote_copy(
                        src_ref=split.at[n], dst_ref=held.at[pos, 2 * turn + core], send_sem=send1.at[n, t],
                        recv_sem=recv1.at[pos, 2 * turn + core], device_id=device_of(g, other, c), device_id_type=MESH,
                    ).start()

    @pl.loop(0, 16)
    def _(i):
        p, s = lax.div(i, 8), lax.rem(i, 8)
        pltpu.make_async_copy(held.at[p, s], held.at[p, s], recv1.at[p, s]).wait()

    diagonal = (k == 1) | (k == 7)
    probe = jnp.where(lax.broadcasted_iota(I32, (8, D), 1) == 0, 1.0, 0.0).astype(BF)

    def bias_of(cols):
        mark = mm(probe, cols, NT)[0:1, :]
        return jnp.where(mark > 2.0, -1e4, 0.0)

    @pl.when(jnp.logical_not(diagonal))
    def _():
        @pl.loop(0, 8)
        def _(b):
            cols = held[0, b]
            bias = bias_of(cols)

            @pl.loop(0, 8)
            def _(a):
                sims = mm(held[1, a], cols, NT) + bias
                acc[1, a] = jnp.maximum(acc[1, a], jnp.maximum(sims[:, :128], sims[:, 128:]))

    @pl.when(diagonal)
    def _():
        for p in range(2):
            @pl.loop(0, 8)
            def _(b):
                cols = held[p, b]
                bias = bias_of(cols)
                ri = lax.broadcasted_iota(I32, (256, 256), 0)
                ci = lax.broadcasted_iota(I32, (256, 256), 1)

                @pl.loop(b, 8)
                def _(a):
                    sims = mm(held[p, a], cols, NT) + bias
                    sims = jnp.where(ci + (b - a) * 256 < ri, sims, -1.0)
                    acc[p, a] = jnp.maximum(acc[p, a], jnp.maximum(sims[:, :128], sims[:, 128:]))

    for p in range(2):
        block = pick(2 * k + p, FLAT_BLOCKS)
        turn = pick(2 * k + p, FLAT_TURN)

        @pl.loop(0, 8)
        def _(a):
            pbest[p, a] = jnp.max(acc[p, a].T, axis=0, keepdims=True)

        for t in range(4):
            other = pick(4 * block + t, FLAT_SHARERS)
            pos = pick(4 * block + t, FLAT_POS)
            for c in range(2):
                mine = (other == k) & (core == c)

                @pl.when(mine)
                def _():
                    pltpu.make_async_copy(pbest.at[p, 2 * t + c], rbest.at[pos, core, turn], recv2.at[pos, core, turn]).start()

                @pl.when(jnp.logical_not(mine))
                def _():
                    pltpu.make_async_remote_copy(
                        src_ref=pbest.at[p, 2 * t + c], dst_ref=rbest.at[pos, core, turn], send_sem=send2.at[p, t, c],
                        recv_sem=recv2.at[pos, core, turn], device_id=device_of(g, other, c), device_id_type=MESH,
                    ).start()

    wi = lax.broadcasted_iota(I32, (128, 128), 0)
    weights = jnp.where(wi == 0, 1.0, jnp.where(wi == 1, 256.0, jnp.where(wi == 2, 2048.0, 0.0))).astype(BF)
    slot_all = mm(arrived[...].reshape(ROWS, WIDE)[:, D:WIDE], weights).astype(I32)
    sub = lax.broadcasted_iota(I32, (ROWS, 128), 0) & 7
    lanes = lax.broadcasted_iota(I32, (ROWS, 128), 1)
    slot_all = jnp.where(slot_all >= 2048, slot_all - 2048 + (sub >> 2) * 512, -1)

    @pl.loop(0, 16)
    def _(i):
        p, c, t = lax.div(i, 8), lax.rem(lax.div(i, 4), 2), lax.rem(i, 4)
        pltpu.make_async_copy(rbest.at[p, c, t], rbest.at[p, c, t], recv2.at[p, c, t]).wait()

    value = jnp.full((ROWS, 128), -1.0, F32)
    for b in range(2):
        for c in range(2):
            best = jnp.maximum(
                jnp.maximum(rbest[b, c, 0], rbest[b, c, 1]), jnp.maximum(rbest[b, c, 2], rbest[b, c, 3])
            )
            for e in range(2):
                at = lanes + (b * 512 + c * 256 + e * 128)
                value = jnp.where(slot_all == at, best[:, e * 128 : (e + 1) * 128], value)
    value = jnp.max(value, axis=1, keepdims=True)
    value = jnp.where(lanes == sub, value, -1.0).reshape(DEVS, 8, 128)
    rep[...] = jnp.max(value, axis=1, keepdims=True)

    pltpu.make_async_copy(rep.at[me], back.at[me], recv3).start()

    @pl.loop(1, DEVS)
    def _(j):
        d = lax.rem(me + 37 * j, DEVS)
        pltpu.make_async_remote_copy(
            src_ref=rep.at[d], dst_ref=back.at[me], send_sem=send3, recv_sem=recv3,
            device_id=(lax.div(d, 16), lax.rem(d, 16)), device_id_type=MESH,
        ).start()

    pltpu.make_async_copy(back, back, recv3).wait()
    mine = jnp.broadcast_to(back[...], (DEVS, 8, 128)).reshape(ROWS, 128)
    mine = jnp.max(jnp.where(lanes == sub, mine, -1.0), axis=1, keepdims=True)
    line = lax.broadcasted_iota(I32, (ROWS, 128), 0)
    for i in range(8):
        part = slice(i * 128, (i + 1) * 128)
        out_ref[:, part] = jnp.max(jnp.where(line == send_at[:, part], mine, -1.0), axis=0, keepdims=True)

    some = packed.at[pl.ds(0, DEVS - 1)]
    pltpu.make_async_copy(some, some, send0).wait()
    some = rep.at[pl.ds(0, DEVS - 1)]
    pltpu.make_async_copy(some, some, send3).wait()
    for b in range(2):
        block = pick(2 * k + b, FLAT_BLOCKS)
        for t in range(4):
            other = pick(4 * block + t, FLAT_SHARERS)
            for c in range(2):
                @pl.when(jnp.logical_not((other == k) & (core == c)))
                def _():
                    pltpu.make_async_copy(split.at[2 * b + c], split.at[2 * b + c], send1.at[2 * b + c, t]).wait()
                    pltpu.make_async_copy(pbest.at[b, 2 * t + c], pbest.at[b, 2 * t + c], send2.at[b, t, c]).wait()


def on_device(embeddings, cluster, rank):
    vmem = pl.BlockSpec(memory_space=pltpu.VMEM)
    out = pl.pallas_call(
        kernel,
        out_shape=jax.ShapeDtypeStruct((1, ROWS), F32),
        in_specs=[vmem] * 3,
        out_specs=vmem,
        scratch_shapes=[
            pltpu.VMEM((ROWS, D), BF),
            pltpu.VMEM((DEVS, 8, WIDE), BF),
            pltpu.VMEM((DEVS, 8, WIDE), BF),
            pltpu.VMEM((4, HALF, D), BF),
            pltpu.VMEM((2, 8, HALF, D), BF),
            pltpu.VMEM((2, 8, HALF, 128), F32),
            pltpu.VMEM((2, 8, 1, HALF), F32),
            pltpu.VMEM((2, 2, 4, 1, HALF), F32),
            pltpu.VMEM((DEVS, 1, 128), F32),
            pltpu.VMEM((DEVS, 1, 128), F32),
            pltpu.SemaphoreType.DMA,
            pltpu.SemaphoreType.DMA,
            pltpu.SemaphoreType.DMA((4, 4)),
            pltpu.SemaphoreType.DMA((2, 8)),
            pltpu.SemaphoreType.DMA((2, 4, 2)),
            pltpu.SemaphoreType.DMA((2, 2, 4)),
            pltpu.SemaphoreType.DMA,
            pltpu.SemaphoreType.DMA,
        ],
        compiler_params=pltpu.CompilerParams(
            collective_id=0, has_side_effects=True, vmem_limit_bytes=56 * 2**20
        ),
        cost_estimate=pl.CostEstimate(flops=12_000_000_000, bytes_accessed=2_000_000, transcendentals=1024),
    )(embeddings, cluster.reshape(1, -1), rank.reshape(1, -1))
    return out.reshape(-1)


def solution(mesh):
    in_specs = (P(("grp", "mem"), None), P(("grp", "mem")), P(("grp", "mem")))
    out_specs = P(("grp", "mem"))
    return jax.shard_map(
        on_device, mesh=mesh, in_specs=in_specs, out_specs=out_specs, check_vma=False
    )
```

time: 401 us -> 145 us (0.36)
  waiting for transfers between devices: 149 us -> 0 us
  Pallas kernels: 0 us -> 144 us
  blocking collectives: 69.6 us -> 0 us
  local copies, waits for them, and re-layouts: 70.5 us -> 1.28 us
  loops' own time: 43.2 us -> 0 us
  other arithmetic: 32.3 us -> 0 us
  starting transfers between devices: 19.2 us -> 0 us
  between operations: 13.6 us -> 0.01 us
    pallas_call x0 -> x1, Pallas kernels: none -> 144 us  [on_device(): pl.pallas_call(kernel, out_shape=jax.ShapeDtypeStruct((1, ROWS), F32), in...]
    all_gather x1 -> x0, waiting for transfers between devices: 124 us -> none  [on_device(): cols_all = lax.all_gather(grid, 'mem', axis=1, tiled=True)]
    all_to_all x1 -> x0, blocking collectives: 50.3 us -> none  [on_device(): lax.all_to_all(reply, ('grp', 'mem'), split_axis=0, concat_axis=0, tiled=...]
    another operation x65 -> x0, loops' own time: 43.2 us -> none  [the longest x1 41.9 us: on_device(): best = lax.fori_loop(0, span // half, one_tile, initial)]
    dynamic_slice x64 -> x0, local copies, waits for them, and re-layouts: 38.6 us -> none  [the longest x32 38.2 us: one_tile(): cols = lax.dynamic_slice_in_dim(cols_all, step * half, half, 1)]
    all_to_all x2 -> x0, waiting for transfers between devices: 24.7 us -> none  [the longest x1 22.6 us: on_device(): lax.all_to_all(outgoing, ('grp', 'mem'), split_axis=0, concat_axis=0, til...]
    add x35 -> x0, other arithmetic: 21.2 us -> none  [the longest x32 21.2 us: column_ranks(): half_of(spots // slot_dev, spots % slot_dev // half) * half + spots % half]
    all_gather x1 -> x0, blocking collectives: 19.3 us -> none  [on_device(): live_all = lax.all_gather(present, 'mem', axis=1, tiled=True)]
  transfers between devices with their start and end apart: 3 -> 0, of which waited for: 3 -> 0; matrix products, arithmetic and copies ran while one was open for 4% -> 0% of each run, Pallas kernels for 0% -> 0%
where the time goes in v1:
time: 145 us
  Pallas kernels  144 us (99%)
    pallas_call x1, Pallas kernels, on_device(): pl.pallas_call(kernel, out_shape=jax.ShapeDtypeStruct((1, ROWS), F32), in...  144 us

profile of v1, /device:TPU:1, one launch (start us, length us, event | category | flops | bytes accessed | tf_op | source)
XLA Modules:
  0.0 145.3 jit_solution(16720673331977703993)
XLA Ops:
  0.0 144.0 %shard_map.37 = f32[1,1024]{1,0:T(1,128)} custom-call(bf16[1024,768]{1,0:T(8,128)(2,1)} %emb_ref.1, s32[1,1024]{1,0:T(1,128)} %bitcast.4, s32[1,1024]{1,0:T(1,128)} %bitcast.5), custom_call_target="tpu_custom_call" | custom-call | flops 12000000000 | bytes 2000000 | tf_op jit(solution)/shard_map/pallas_call | solution.py:306
  144.0 1.3 copy.5

commit v2 on v1

--- a/solution.py
+++ b/solution.py
@@ -17,9 +17,10 @@
 F32 = jnp.float32
 I32 = jnp.int32
 
-BLOCKS = ((0, 1), (0, 1), (0, 2), (0, 3), (1, 2), (1, 3), (2, 3), (2, 3))
-SHARERS = ((0, 1, 2, 3), (0, 1, 4, 5), (2, 4, 6, 7), (3, 5, 6, 7))
-PLACE = ((3, 1, 1), (3, 0, 1), (0, 1, 1), (2, 0, 1), (0, 1, 0), (2, 0, 0), (1, 1, 0), (1, 0, 0))
+BLOCKS = ((0, 1), (0, 1), (0, 2), (1, 2), (0, 3), (1, 3), (2, 3), (2, 3))
+SHARERS = ((0, 1, 2, 4), (0, 1, 3, 5), (2, 3, 6, 7), (4, 5, 6, 7))
+PLACE = ((1, 1, 0), (0, 2, 1), (2, 1, 1), (3, 1, 2), (1, 2, 0), (0, 1, 1), (2, 2, 1), (3, 2, 2))
+SPOT_OF_CLASS = (0, 6, 7, 2, 3, 1, 4, 5)
 
 
 def pick(index, table):
@@ -38,22 +39,23 @@
     return out
 
 
-def device_of(g, k, core):
-    x = pick(k, [p[0] for p in PLACE])
-    y = lax.rem(pick(k, [p[1] for p in PLACE]) + lax.div(g, 2), 4)
-    z = lax.rem(pick(k, [p[2] for p in PLACE]) + lax.rem(lax.div(g, 2), 2) + 2 * lax.rem(g, 2), 4)
-    return 2 * x + core, 4 * z + y
+def device_of(g, c, u):
+    spot = 4 * c + lax.div(u, 2)
+    turn = lax.div(g, 2)
+    x = lax.rem(pick(spot, [p[0] for p in PLACE]) + turn, 4)
+    y = lax.rem(pick(spot, [p[1] for p in PLACE]) + turn, 4)
+    z = lax.rem(pick(spot, [p[2] for p in PLACE]) + 2 * lax.rem(g, 2), 4)
+    return 2 * x + lax.rem(u, 2), 4 * z + y
 
 
 def my_place():
     grp, mem = lax.axis_index("grp"), lax.axis_index("mem")
     x, core = lax.div(grp, 2), lax.rem(grp, 2)
     z, y = lax.div(mem, 4), lax.rem(mem, 4)
-    odd = lax.rem(y + z, 2)
-    k = pick(2 * x + odd, [2, 4, 7, 6, 5, 3, 0, 1])
-    gy = lax.rem(y - pick(k, [p[1] for p in PLACE]) + 4, 4)
-    gz = lax.rem(z - pick(k, [p[2] for p in PLACE]) - lax.rem(gy, 2) + 8, 4)
-    return grp, mem, 2 * gy + lax.div(gz, 2), k, core
+    spot = pick(2 * lax.rem(x - y + 4, 4) + lax.rem(z, 2), SPOT_OF_CLASS)
+    turn = lax.rem(x - pick(spot, [p[0] for p in PLACE]) + 4, 4)
+    g = 2 * turn + lax.div(lax.rem(z - pick(spot, [p[2] for p in PLACE]) + 4, 4), 2)
+    return grp, mem, g, lax.div(spot, 4), 2 * lax.rem(spot, 4) + core, core
 
 
 FLAT_SHARERS = [k for row in SHARERS for k in row]
@@ -61,6 +63,8 @@
 FLAT_BLOCKS = [b for pair in BLOCKS for b in pair]
 FLAT_TURN = [SHARERS[BLOCKS[k][p]].index(k) for k in range(8) for p in range(2)]
 
+FLOW = 6
+
 NT = (((1,), (1,)), ((), ()))
 NN = (((1,), (0,)), ((), ()))
 
@@ -69,9 +73,13 @@
     return lax.dot_general(a, b, dims, preferred_element_type=F32)
 
 
+def goes(block, t, turn):
+    return (lax.rem(turn, 2) == t % 2) | ((block < 2) & (t >= 2))
+
+
 def kernel(emb_ref, clu_ref, rank_ref, out_ref, unit, packed, arrived, split, held, acc, pbest,
-           rbest, rep, back, send0, recv0, send1, recv1, send2, recv2, send3, recv3):
-    grp, mem, g, k, core = my_place()
+           rbest, rep, back, bias, send0, recv0, send1, recv1, send2, recv2, send3, recv3, send4):
+    grp, mem, g, mine_c, k, core = my_place()
     me = grp * 16 + mem
 
     barrier = pltpu.get_barrier_semaphore()
@@ -95,10 +103,11 @@
     share = ((vh >> 3) << 2) + ((vh & 7) >> 1)
     vk = pick_vec(share, FLAT_SHARERS)
     vp = pick_vec(share, FLAT_POS)
-    vx = pick_vec(vk, [p[0] for p in PLACE])
-    vy = (pick_vec(vk, [p[1] for p in PLACE]) + (vg >> 1)) & 3
-    vz = (pick_vec(vk, [p[2] for p in PLACE]) + ((vg >> 1) & 1) + 2 * (vg & 1)) & 3
-    vdev = (2 * vx + (vh & 1)) * 16 + 4 * vz + vy
+    vs = 4 * (vh & 1) + (vk >> 1)
+    vx = (pick_vec(vs, [p[0] for p in PLACE]) + (vg >> 1)) & 3
+    vy = (pick_vec(vs, [p[1] for p in PLACE]) + (vg >> 1)) & 3
+    vz = (pick_vec(vs, [p[2] for p in PLACE]) + 2 * (vg & 1)) & 3
+    vdev = (2 * vx + (vk & 1)) * 16 + 4 * vz + vy
     bucket = jnp.where(alive, 2 * vdev + vp, -1)
     low = lax.broadcasted_iota(I32, (128, 256), 0)
     col = lax.broadcasted_iota(I32, (128, 256), 1)
@@ -165,58 +174,101 @@
             for t in range(4):
                 other = pick(4 * block + t, FLAT_SHARERS)
                 pos = pick(4 * block + t, FLAT_POS)
-                mine = (other == k) & (core == c)
+                wanted = goes(block, t, turn)
+                mine = (other == k) & (mine_c == c)
+                slot = 2 * turn + mine_c
 
                 @pl.when(mine)
                 def _():
-                    pltpu.make_async_copy(split.at[n], held.at[pos, 2 * turn + core], recv1.at[pos, 2 * turn + core]).start()
-
-                @pl.when(jnp.logical_not(mine))
+                    pltpu.make_async_copy(split.at[n], held.at[pos, slot], recv1.at[pos, slot]).start()
+
+                @pl.when(wanted & jnp.logical_not(mine))
                 def _():
                     pltpu.make_async_remote_copy(
-                        src_ref=split.at[n], dst_ref=held.at[pos, 2 * turn + core], send_sem=send1.at[n, t],
-                        recv_sem=recv1.at[pos, 2 * turn + core], device_id=device_of(g, other, c), device_id_type=MESH,
+                        src_ref=split.at[n], dst_ref=held.at[pos, slot], send_sem=send1.at[n, t],
+                        recv_sem=recv1.at[pos, slot], device_id=device_of(g, c, other), device_id_type=MESH,
                     ).start()
 
-    @pl.loop(0, 16)
-    def _(i):
-        p, s = lax.div(i, 8), lax.rem(i, 8)
-        pltpu.make_async_copy(held.at[p, s], held.at[p, s], recv1.at[p, s]).wait()
-
     diagonal = (k == 1) | (k == 7)
+    both = (k < 2) | (k >= 6)
     probe = jnp.where(lax.broadcasted_iota(I32, (8, D), 1) == 0, 1.0, 0.0).astype(BF)
 
-    def bias_of(cols):
-        mark = mm(probe, cols, NT)[0:1, :]
-        return jnp.where(mark > 2.0, -1e4, 0.0)
-
-    @pl.when(jnp.logical_not(diagonal))
-    def _():
-        @pl.loop(0, 8)
-        def _(b):
-            cols = held[0, b]
-            bias = bias_of(cols)
-
-            @pl.loop(0, 8)
+    def passes(p, s):
+        yes = lax.rem(lax.div(s, 2), 2) == core
+        return yes if p else yes & both
+
+    def arrive(s):
+        for p in range(2):
+            pltpu.make_async_copy(held.at[p, s], held.at[p, s], recv1.at[p, s]).wait()
+
+            @pl.when(passes(p, s))
+            def _():
+                pltpu.make_async_remote_copy(
+                    src_ref=held.at[p, s], dst_ref=held.at[p, s], send_sem=send4.at[p, s], recv_sem=recv1.at[p, s],
+                    device_id=(grp + 1 - 2 * core, mem), device_id_type=MESH,
+                ).start()
+
+        for p in range(2):
+            mark = mm(probe, held[p, s], NT)[0:1, :]
+            bias[p, s] = jnp.where(mark > 2.0, -1e4, 0.0)
+
+    def tile(pr, a, pc, b, below=None):
+        sims = mm(held[pr, a], held[pc, b], NT) + bias[pc, b]
+        if below is not None:
+            sims = jnp.where(below, sims, -1.0)
+        acc[pr, a] = jnp.maximum(acc[pr, a], jnp.maximum(sims[:, :128], sims[:, 128:]))
+
+    @pl.loop(0, FLOW)
+    def _(s):
+        arrive(s)
+
+        @pl.when(jnp.logical_not(diagonal))
+        def _():
+            @pl.loop(0, s + 1)
             def _(a):
-                sims = mm(held[1, a], cols, NT) + bias
-                acc[1, a] = jnp.maximum(acc[1, a], jnp.maximum(sims[:, :128], sims[:, 128:]))
-
-    @pl.when(diagonal)
-    def _():
-        for p in range(2):
-            @pl.loop(0, 8)
+                tile(1, a, 0, s)
+
+            @pl.loop(0, s)
             def _(b):
-                cols = held[p, b]
-                bias = bias_of(cols)
-                ri = lax.broadcasted_iota(I32, (256, 256), 0)
-                ci = lax.broadcasted_iota(I32, (256, 256), 1)
-
-                @pl.loop(b, 8)
-                def _(a):
-                    sims = mm(held[p, a], cols, NT) + bias
-                    sims = jnp.where(ci + (b - a) * 256 < ri, sims, -1.0)
-                    acc[p, a] = jnp.maximum(acc[p, a], jnp.maximum(sims[:, :128], sims[:, 128:]))
+                tile(1, s, 0, b)
+
+        @pl.when(diagonal)
+        def _():
+            for p in range(2):
+                @pl.loop(0, s)
+                def _(b):
+                    tile(p, s, p, b)
+
+                tile(p, s, p, s, lax.broadcasted_iota(I32, (256, 256), 1) < lax.broadcasted_iota(I32, (256, 256), 0))
+
+    for s in range(FLOW, 8):
+        arrive(s)
+
+        @pl.when(jnp.logical_not(diagonal))
+        def _():
+            sims = mm(held[1, 0 : s + 1].reshape((s + 1) * 256, D), held[0, s], NT) + bias[0, s]
+            sims = jnp.maximum(sims[:, :128], sims[:, 128:]).reshape(s + 1, 256, 128)
+            acc[1, 0 : s + 1] = jnp.maximum(acc[1, 0 : s + 1], sims)
+            sims = mm(held[1, s], held[0, 0:s].reshape(s * 256, D), NT)
+            top = acc[1, s]
+            for b in range(s):
+                one = sims[:, b * 256 : (b + 1) * 256] + bias[0, b]
+                top = jnp.maximum(top, jnp.maximum(one[:, :128], one[:, 128:]))
+            acc[1, s] = top
+
+        @pl.when(diagonal)
+        def _():
+            @pl.loop(0, 2)
+            def _(p):
+                sims = mm(held[p, s], held[p, 0 : s + 1].reshape((s + 1) * 256, D), NT)
+                top = acc[p, s]
+                for b in range(s + 1):
+                    one = sims[:, b * 256 : (b + 1) * 256] + bias[p, b]
+                    if b == s:
+                        below = lax.broadcasted_iota(I32, (256, 256), 1) < lax.broadcasted_iota(I32, (256, 256), 0)
+                        one = jnp.where(below, one, -1.0)
+                    top = jnp.maximum(top, jnp.maximum(one[:, :128], one[:, 128:]))
+                acc[p, s] = top
 
     for p in range(2):
         block = pick(2 * k + p, FLAT_BLOCKS)
@@ -230,17 +282,19 @@
             other = pick(4 * block + t, FLAT_SHARERS)
             pos = pick(4 * block + t, FLAT_POS)
             for c in range(2):
-                mine = (other == k) & (core == c)
+                mine = (other == k) & (mine_c == c)
+                to = rbest.at[pos, mine_c, turn]
+                sem = recv2.at[pos, mine_c, turn]
 
                 @pl.when(mine)
                 def _():
-                    pltpu.make_async_copy(pbest.at[p, 2 * t + c], rbest.at[pos, core, turn], recv2.at[pos, core, turn]).start()
+                    pltpu.make_async_copy(pbest.at[p, 2 * t + c], to, sem).start()
 
                 @pl.when(jnp.logical_not(mine))
                 def _():
                     pltpu.make_async_remote_copy(
-                        src_ref=pbest.at[p, 2 * t + c], dst_ref=rbest.at[pos, core, turn], send_sem=send2.at[p, t, c],
-                        recv_sem=recv2.at[pos, core, turn], device_id=device_of(g, other, c), device_id_type=MESH,
+                        src_ref=pbest.at[p, 2 * t + c], dst_ref=to, send_sem=send2.at[p, t, c],
+                        recv_sem=sem, device_id=device_of(g, c, other), device_id_type=MESH,
                     ).start()
 
     wi = lax.broadcasted_iota(I32, (128, 128), 0)
@@ -292,13 +346,25 @@
     pltpu.make_async_copy(some, some, send3).wait()
     for b in range(2):
         block = pick(2 * k + b, FLAT_BLOCKS)
+        turn = pick(2 * k + b, FLAT_TURN)
         for t in range(4):
             other = pick(4 * block + t, FLAT_SHARERS)
             for c in range(2):
-                @pl.when(jnp.logical_not((other == k) & (core == c)))
+                away = jnp.logical_not((other == k) & (mine_c == c))
+
+                @pl.when(away & goes(block, t, turn))
                 def _():
                     pltpu.make_async_copy(split.at[2 * b + c], split.at[2 * b + c], send1.at[2 * b + c, t]).wait()
+
+                @pl.when(away)
+                def _():
                     pltpu.make_async_copy(pbest.at[b, 2 * t + c], pbest.at[b, 2 * t + c], send2.at[b, t, c]).wait()
+
+        @pl.loop(0, 8)
+        def _(s):
+            @pl.when(passes(b, s))
+            def _():
+                pltpu.make_async_copy(held.at[b, s], held.at[b, s], send4.at[b, s]).wait()
 
 
 def on_device(embeddings, cluster, rank):
@@ -319,6 +385,7 @@
             pltpu.VMEM((2, 2, 4, 1, HALF), F32),
             pltpu.VMEM((DEVS, 1, 128), F32),
             pltpu.VMEM((DEVS, 1, 128), F32),
+            pltpu.VMEM((2, 8, 1, HALF), F32),
             pltpu.SemaphoreType.DMA,
             pltpu.SemaphoreType.DMA,
             pltpu.SemaphoreType.DMA((4, 4)),
@@ -327,6 +394,7 @@
             pltpu.SemaphoreType.DMA((2, 2, 4)),
             pltpu.SemaphoreType.DMA,
             pltpu.SemaphoreType.DMA,
+            pltpu.SemaphoreType.DMA((2, 8)),
         ],
         compiler_params=pltpu.CompilerParams(
             collective_id=0, has_side_effects=True, vmem_limit_bytes=56 * 2**20

time: 145 us -> 146 us (level)
  no operation moved by 1% of the time
where the time goes in v2:
time: 146 us
  Pallas kernels  144 us (99%)
    pallas_call x1, Pallas kernels, on_device(): pl.pallas_call(kernel, out_shape=jax.ShapeDtypeStruct((1, ROWS), F32), in...  144 us

profile of v2, /device:TPU:1, one launch (start us, length us, event | category | flops | bytes accessed | tf_op | source)
XLA Modules:
  0.0 145.5 jit_solution(16832751629995184014)
XLA Ops:
  0.0 144.2 %shard_map.37 = f32[1,1024]{1,0:T(1,128)} custom-call(bf16[1024,768]{1,0:T(8,128)(2,1)} %emb_ref.1, s32[1,1024]{1,0:T(1,128)} %bitcast.4, s32[1,1024]{1,0:T(1,128)} %bitcast.5), custom_call_target="tpu_custom_call" | custom-call | flops 12000000000 | bytes 2000000 | tf_op jit(solution)/shard_map/pallas_call | solution.py:372
  144.2 1.3 copy.5

commit v3 on v2

--- a/solution.py
+++ b/solution.py
@@ -63,6 +63,7 @@
 FLAT_BLOCKS = [b for pair in BLOCKS for b in pair]
 FLAT_TURN = [SHARERS[BLOCKS[k][p]].index(k) for k in range(8) for p in range(2)]
 
+PIECES = 16
 FLOW = 6
 
 NT = (((1,), (1,)), ((), ()))
@@ -74,7 +75,7 @@
 
 
 def goes(block, t, turn):
-    return (lax.rem(turn, 2) == t % 2) | ((block < 2) & (t >= 2))
+    return (lax.rem(turn, 2) == lax.rem(t, 2)) | ((block < 2) & (t >= 2))
 
 
 def kernel(emb_ref, clu_ref, rank_ref, out_ref, unit, packed, arrived, split, held, acc, pbest,
@@ -171,23 +172,34 @@
             here = rows[:, D + 2 : D + 3]
             split[n, :, 0:128] = jnp.where(first & (here < 0.5), 256.0, rows[:, 0:128]).astype(BF)
             split[n, :, 128:D] = rows[:, 128:D].astype(BF)
-            for t in range(4):
+
+    for b in range(2):
+        turn = pick(2 * k + b, FLAT_TURN)
+        slot = 2 * turn + mine_c
+        pltpu.make_async_copy(split.at[2 * b + mine_c], held.at[b, slot], recv1.at[b, slot]).start()
+
+    @pl.loop(0, PIECES)
+    def _(piece):
+        rows = pl.ds(pl.multiple_of(piece * (HALF // PIECES), HALF // PIECES), HALF // PIECES)
+        for step in range(4):
+            for b in range(2):
+                block = pick(2 * k + b, FLAT_BLOCKS)
+                turn = pick(2 * k + b, FLAT_TURN)
+                t = lax.rem(turn + step, 4)
                 other = pick(4 * block + t, FLAT_SHARERS)
                 pos = pick(4 * block + t, FLAT_POS)
-                wanted = goes(block, t, turn)
-                mine = (other == k) & (mine_c == c)
                 slot = 2 * turn + mine_c
-
-                @pl.when(mine)
-                def _():
-                    pltpu.make_async_copy(split.at[n], held.at[pos, slot], recv1.at[pos, slot]).start()
-
-                @pl.when(wanted & jnp.logical_not(mine))
-                def _():
-                    pltpu.make_async_remote_copy(
-                        src_ref=split.at[n], dst_ref=held.at[pos, slot], send_sem=send1.at[n, t],
-                        recv_sem=recv1.at[pos, slot], device_id=device_of(g, c, other), device_id_type=MESH,
-                    ).start()
+                for flip in range(2):
+                    c = lax.rem(mine_c + flip, 2)
+
+                    if step or flip:
+                        @pl.when(goes(block, t, turn))
+                        def _():
+                            pltpu.make_async_remote_copy(
+                                src_ref=split.at[2 * b + c, rows], dst_ref=held.at[pos, slot, rows],
+                                send_sem=send1.at[2 * b + flip, step], recv_sem=recv1.at[pos, slot],
+                                device_id=device_of(g, c, other), device_id_type=MESH,
+                            ).start()
 
     diagonal = (k == 1) | (k == 7)
     both = (k < 2) | (k >= 6)
@@ -347,16 +359,17 @@
     for b in range(2):
         block = pick(2 * k + b, FLAT_BLOCKS)
         turn = pick(2 * k + b, FLAT_TURN)
+        for step in range(4):
+            for flip in range(2):
+                if step or flip:
+                    @pl.when(goes(block, lax.rem(turn + step, 4), turn))
+                    def _():
+                        pltpu.make_async_copy(split.at[0], split.at[0], send1.at[2 * b + flip, step]).wait()
+
         for t in range(4):
             other = pick(4 * block + t, FLAT_SHARERS)
             for c in range(2):
-                away = jnp.logical_not((other == k) & (mine_c == c))
-
-                @pl.when(away & goes(block, t, turn))
-                def _():
-                    pltpu.make_async_copy(split.at[2 * b + c], split.at[2 * b + c], send1.at[2 * b + c, t]).wait()
-
-                @pl.when(away)
+                @pl.when(jnp.logical_not((other == k) & (mine_c == c)))
                 def _():
                     pltpu.make_async_copy(pbest.at[b, 2 * t + c], pbest.at[b, 2 * t + c], send2.at[b, t, c]).wait()
 

time: 146 us -> 121 us (0.83)
  Pallas kernels: 144 us -> 120 us
    pallas_call x1, Pallas kernels: 144 us -> 120 us  [on_device(): pl.pallas_call(kernel, out_shape=jax.ShapeDtypeStruct((1, ROWS), F32), in...]
where the time goes in v3:
time: 121 us
  Pallas kernels  120 us (99%)
  local copies, waits for them, and re-layouts  1.28 us (1%)
    pallas_call x1, Pallas kernels, on_device(): pl.pallas_call(kernel, out_shape=jax.ShapeDtypeStruct((1, ROWS), F32), in...  120 us

profile of v3, /device:TPU:1, one launch (start us, length us, event | category | flops | bytes accessed | tf_op | source)
XLA Modules:
  0.0 121.0 jit_solution(10036362420881643863)
XLA Ops:
  0.0 119.8 %shard_map.37 = f32[1,1024]{1,0:T(1,128)} custom-call(bf16[1024,768]{1,0:T(8,128)(2,1)} %emb_ref.1, s32[1,1024]{1,0:T(1,128)} %bitcast.4, s32[1,1024]{1,0:T(1,128)} %bitcast.5), custom_call_target="tpu_custom_call" | custom-call | flops 12000000000 | bytes 2000000 | tf_op jit(solution)/shard_map/pallas_call | solution.py:385
  119.8 1.3 %copy.5 = f32[1024]{0:T(1024)} copy(f32[1024]{0:T(1024)} %bitcast.3) | data formatting | bytes 8192

commit v4 on v3

v4 whole, which is shorter than its diff:
```python
import functools

import jax
import jax.numpy as jnp
from jax import lax
from jax.experimental import pallas as pl
from jax.experimental.pallas import tpu as pltpu
from jax.sharding import PartitionSpec as P

MESH = pl.DeviceIdType.MESH
D = 768
PART = 384
ROWS = 1024
HALF = 256
DEVS = 128
BF = jnp.bfloat16
F32 = jnp.float32
I32 = jnp.int32

BLOCKS = ((0, 1), (0, 1), (0, 2), (1, 2), (0, 3), (1, 3), (2, 3), (2, 3))
SHARERS = ((0, 2, 1, 4), (1, 3, 0, 5), (6, 7, 2, 3), (4, 5, 6, 7))
PLACE = ((1, 1, 0), (0, 2, 1), (2, 1, 1), (3, 1, 2), (1, 2, 0), (0, 1, 1), (2, 2, 1), (3, 2, 2))
SPOT_OF_CLASS = (0, 6, 7, 2, 3, 1, 4, 5)


def pick(index, table):
    out = jnp.int32(table[0])
    for at, value in enumerate(table):
        if at:
            out = jnp.where(index == at, jnp.int32(value), out)
    return out


def pick_vec(index, table):
    out = jnp.full_like(index, table[0])
    for at, value in enumerate(table):
        if at:
            out = jnp.where(index == at, jnp.int32(value), out)
    return out


def device_of(g, c, u):
    spot = 4 * c + lax.div(u, 2)
    turn = lax.div(g, 2)
    x = lax.rem(pick(spot, [p[0] for p in PLACE]) + turn, 4)
    y = lax.rem(pick(spot, [p[1] for p in PLACE]) + turn, 4)
    z = lax.rem(pick(spot, [p[2] for p in PLACE]) + 2 * lax.rem(g, 2), 4)
    return 2 * x + lax.rem(u, 2), 4 * z + y


def my_place():
    grp, mem = lax.axis_index("grp"), lax.axis_index("mem")
    x, core = lax.div(grp, 2), lax.rem(grp, 2)
    z, y = lax.div(mem, 4), lax.rem(mem, 4)
    spot = pick(2 * lax.rem(x - y + 4, 4) + lax.rem(z, 2), SPOT_OF_CLASS)
    turn = lax.rem(x - pick(spot, [p[0] for p in PLACE]) + 4, 4)
    g = 2 * turn + lax.div(lax.rem(z - pick(spot, [p[2] for p in PLACE]) + 4, 4), 2)
    return grp, mem, g, lax.div(spot, 4), 2 * lax.rem(spot, 4) + core, core


FLAT_SHARERS = [k for row in SHARERS for k in row]
FLAT_POS = [BLOCKS[k].index(b) for b in range(4) for k in SHARERS[b]]
FLAT_BLOCKS = [b for pair in BLOCKS for b in pair]
PHASE_POS = [p for k in range(8) for p in sorted((0, 1), key=lambda p: SHARERS[BLOCKS[k][p]].index(k))]
PHASE_BLOCK = [BLOCKS[k][PHASE_POS[2 * k + f]] for k in range(8) for f in range(2)]
PHASE_TURN = [SHARERS[PHASE_BLOCK[2 * k + f]].index(k) for k in range(8) for f in range(2)]
BLOCK_TURN = [SHARERS[BLOCKS[k][p]].index(k) for k in range(8) for p in range(2)]
FLAT_PHASE = [t // 2 for b in range(4) for t in range(4)]

PIECES = 16
NT = (((1,), (1,)), ((), ()))
NN = (((1,), (0,)), ((), ()))


def mm(a, b, dims=NN):
    return lax.dot_general(a, b, dims, preferred_element_type=F32)


def goes(block, other, core):
    return (lax.rem(other, 2) == core) | ((block < 2) & (other >= 2))


def kernel(emb_ref, clu_ref, rank_ref, out_ref, unit, packed, arrived, tag_out, tag_in, split, held, acc, pbest,
           rbest, rep, back, bias, send0, recv0, send1, recv1, send2, recv2, send3, recv3, send4, send5, recv5):
    grp, mem, g, mine_c, k, core = my_place()
    me = grp * 16 + mem
    rbest[...] = jnp.full(rbest.shape, -1.0, F32)

    barrier = pltpu.get_barrier_semaphore()

    @pl.loop(1, DEVS)
    def _(j):
        d = lax.rem(me + j, DEVS)
        pl.semaphore_signal(barrier, inc=1, device_id=(lax.div(d, 16), lax.rem(d, 16)), device_id_type=MESH)

    @pl.loop(0, 4)
    def _(i):
        rows = pl.ds(pl.multiple_of(i * 256, 256), 256)
        wide = emb_ref[rows, :].astype(F32)
        total = jnp.sum(wide * wide, axis=1, keepdims=True)
        unit[rows, :] = (wide * lax.rsqrt(total + 1e-06)).astype(BF)

    clu, rank = clu_ref[...], rank_ref[...]
    alive = clu >= 0
    vg = clu >> 1
    vh = rank >> 8
    share = ((vh >> 3) << 2) + ((vh & 7) >> 1)
    vk = pick_vec(share, FLAT_SHARERS)
    vp = pick_vec(share, FLAT_PHASE)
    vs = 4 * (vh & 1) + (vk >> 1)
    vx = (pick_vec(vs, [p[0] for p in PLACE]) + (vg >> 1)) & 3
    vy = (pick_vec(vs, [p[1] for p in PLACE]) + (vg >> 1)) & 3
    vz = (pick_vec(vs, [p[2] for p in PLACE]) + 2 * (vg & 1)) & 3
    vdev = (2 * vx + (vk & 1)) * 16 + 4 * vz + vy
    bucket = jnp.where(alive, 2 * vdev + vp, -1)
    low = lax.broadcasted_iota(I32, (128, 256), 0)
    col = lax.broadcasted_iota(I32, (128, 256), 1)
    tri = jnp.where((low < col) | (col >= 128), 1.0, 0.0).astype(BF)
    carry = jnp.zeros((256, 128), F32)
    bid = lax.broadcasted_iota(I32, (256, 128), 0)
    spots = []
    for i in range(8):
        hit = bid == bucket[:, i * 128 : (i + 1) * 128]
        counts = mm(jnp.where(hit, 1.0, 0.0).astype(BF), tri)
        spots.append(jnp.sum(jnp.where(hit, counts[:, :128] + carry, 0.0), axis=0, keepdims=True))
        carry = carry + counts[:, 128:]
    spot = jnp.concatenate(spots, axis=1).astype(I32)
    send_at = jnp.where(alive, bucket * 4 + spot, -1)

    kind = lax.broadcasted_iota(I32, (256, ROWS), 0)
    labels = jnp.where(kind < 128, (rank & 255).astype(F32), (clu & 1).astype(F32) + 2.0).astype(BF)
    own_lane = lax.broadcasted_iota(I32, (32, 8, 128), 2) == lax.broadcasted_iota(I32, (32, 8, 128), 1)

    @pl.loop(0, 4)
    def _(i):
        line = lax.broadcasted_iota(I32, (256, ROWS), 0) + i * 256
        where_to = jnp.where(line == send_at, 1.0, 0.0).astype(BF)
        code = mm(where_to, labels, NT)
        code = (code[:, :128] + 256.0 * code[:, 128:]).reshape(32, 8, 128)
        devs = pl.ds(pl.multiple_of(i * 32, 32), 32)
        tag_out[devs] = jnp.sum(jnp.where(own_lane, code, 0.0), axis=1, keepdims=True)

    def pack(f):
        @pl.loop(0, 2)
        def _(i):
            at = lax.broadcasted_iota(I32, (512, ROWS), 0)
            line = ((at >> 3) + i * 64) * 8 + f * 4 + (at & 3)
            where_to = jnp.where(line == send_at, 1.0, 0.0).astype(BF)
            front = (lax.broadcasted_iota(I32, (512, PART), 0) & 7) < 4
            rows = jnp.where(front, mm(where_to, unit[:, 0:PART]), mm(where_to, unit[:, PART:D]))
            packed[f, pl.ds(pl.multiple_of(i * 64, 64), 64)] = rows.reshape(64, 8, PART).astype(BF)

    def ship(src, dst, d, ssem, rsem):
        pltpu.make_async_remote_copy(
            src_ref=src, dst_ref=dst, send_sem=ssem, recv_sem=rsem,
            device_id=(lax.div(d, 16), lax.rem(d, 16)), device_id_type=MESH,
        ).start()

    pack(0)
    pl.semaphore_wait(barrier, DEVS - 1)

    pltpu.make_async_copy(tag_out.at[me], tag_in.at[me], recv5).start()
    pltpu.make_async_copy(packed.at[0, me], arrived.at[0, me], recv0.at[0]).start()

    @pl.loop(1, DEVS)
    def _(j):
        d = lax.rem(me + 37 * j, DEVS)
        ship(tag_out.at[d], tag_in.at[me], d, send5, recv5)
        ship(packed.at[0, d], arrived.at[0, me], d, send0.at[0], recv0.at[0])

    pack(1)
    pltpu.make_async_copy(packed.at[1, me], arrived.at[1, me], recv0.at[1]).start()

    @pl.loop(1, DEVS)
    def _(j):
        d = lax.rem(me + 37 * j, DEVS)
        ship(packed.at[1, d], arrived.at[1, me], d, send0.at[1], recv0.at[1])

    acc[...] = jnp.full(acc.shape, -1.0, F32)
    sub8 = lax.broadcasted_iota(I32, (DEVS, 8, 128), 1)
    lane8 = lax.broadcasted_iota(I32, (DEVS, 8, 128), 2)
    pltpu.make_async_copy(tag_in, tag_in, recv5).wait()

    lane = lax.broadcasted_iota(I32, (8, 128), 1)
    weigh = jnp.where(lane == 0, 1.0, jnp.where(lane == 1, 256.0, 0.0)).astype(BF)
    at_half = (lax.broadcasted_iota(I32, (1, ROWS), 1) >> 2) & 1
    lanes = lax.broadcasted_iota(I32, (ROWS, 128), 1)

    def tags(f):
        wide = jnp.broadcast_to(tag_in[...], (DEVS, 8, 128))
        wide = jnp.where(lane8 == f * 4 + (sub8 & 3), wide, 0.0)
        code = jnp.max(wide, axis=2, keepdims=True).reshape(ROWS, 1).astype(I32)
        both = jnp.where(lanes == 0, code & 255, jnp.where(lanes == 1, code >> 8, 0)).astype(F32).astype(BF)
        return mm(weigh, both, NT)[0:1, :].astype(I32) - 512

    slot_rows = [tags(f) for f in range(2)]
    first = lax.broadcasted_iota(I32, (256, 128), 1) == 0

    for f in range(2):
        pltpu.make_async_copy(arrived.at[f], arrived.at[f], recv0.at[f]).wait()
        got = arrived[f].reshape(ROWS, PART)
        for c in range(2):
            line = lax.broadcasted_iota(I32, (256, ROWS), 0) + c * 256
            front = jnp.where(line == jnp.where(at_half == 0, slot_rows[f], -1), 1.0, 0.0)
            rear = jnp.where(line == jnp.where(at_half == 1, slot_rows[f], -1), 1.0, 0.0)
            here = jnp.sum(front, axis=1, keepdims=True)
            rows = mm(front.astype(BF), got)
            split[2 * f + c, :, 0:128] = jnp.where(first & (here < 0.5), 256.0, rows[:, 0:128]).astype(BF)
            split[2 * f + c, :, 128:PART] = rows[:, 128:].astype(BF)
            split[2 * f + c, :, PART:D] = mm(rear.astype(BF), got).astype(BF)

        block = pick(2 * k + f, PHASE_BLOCK)
        turn = pick(2 * k + f, PHASE_TURN)
        slot = 2 * turn + mine_c
        to = held.at[pick(2 * k + f, PHASE_POS), slot]
        pltpu.make_async_copy(split.at[2 * f + mine_c], to, recv1.at[pick(2 * k + f, PHASE_POS), slot]).start()

        @pl.loop(0, PIECES)
        def _(piece):
            rows = pl.ds(pl.multiple_of(piece * (HALF // PIECES), HALF // PIECES), HALF // PIECES)
            for step in range(4):
                t = lax.rem(turn + step, 4)
                other = pick(4 * block + t, FLAT_SHARERS)
                pos = pick(4 * block + t, FLAT_POS)
                for flip in range(2):
                    c = lax.rem(mine_c + flip, 2)

                    if step or flip:
                        @pl.when(goes(block, other, core))
                        def _():
                            pltpu.make_async_remote_copy(
                                src_ref=split.at[2 * f + c, rows], dst_ref=held.at[pos, slot, rows],
                                send_sem=send1.at[2 * f + flip, step], recv_sem=recv1.at[pos, slot],
                                device_id=device_of(g, c, other), device_id_type=MESH,
                            ).start()

    diagonal = (k == 1) | (k == 7)
    both = (k < 2) | (k >= 6)
    probe = jnp.where(lax.broadcasted_iota(I32, (8, D), 1) == 0, 1.0, 0.0).astype(BF)

    def passes(p, s):
        owner = pick(4 * pick(2 * k + p, FLAT_BLOCKS) + lax.div(s, 2), FLAT_SHARERS)
        yes = lax.rem(owner, 2) == core
        return yes if p else yes & both

    def arrive(s):
        for p in range(2):
            pltpu.make_async_copy(held.at[p, s], held.at[p, s], recv1.at[p, s]).wait()

            @pl.when(passes(p, s))
            def _():
                pltpu.make_async_remote_copy(
                    src_ref=held.at[p, s], dst_ref=held.at[p, s], send_sem=send4.at[p, s], recv_sem=recv1.at[p, s],
                    device_id=(grp + 1 - 2 * core, mem), device_id_type=MESH,
                ).start()

        for p in range(2):
            mark = mm(probe, held[p, s], NT)[0:1, :]
            bias[p, s] = jnp.where(mark > 2.0, -1e4, 0.0)

    def compare(pr, lo, hi, pc, b, corner=False):
        n = hi - lo
        sims = mm(held[pr, lo:hi].reshape(n * 256, D), held[pc, b], NT) + bias[pc, b]
        if corner:
            below = lax.broadcasted_iota(I32, (n * 256, 256), 1) < lax.broadcasted_iota(I32, (n * 256, 256), 0)
            sims = jnp.where(below, sims, -1.0)
        sims = jnp.maximum(sims[:, :128], sims[:, 128:]).reshape(n, 256, 128)
        acc[pr, lo:hi] = jnp.maximum(acc[pr, lo:hi], sims)

    @pl.loop(0, 4)
    def _(s):
        arrive(s)

    @pl.when(jnp.logical_not(diagonal))
    def _():
        @pl.loop(0, 4)
        def _(b):
            compare(1, 0, 4, 0, b)

    @pl.when(diagonal)
    def _():
        @pl.loop(0, 2)
        def _(p):
            for b in range(4):
                compare(p, b, 4, p, b, True)

    @pl.loop(4, 8)
    def _(s):
        arrive(s)

    @pl.when(jnp.logical_not(diagonal))
    def _():
        @pl.loop(0, 4)
        def _(b):
            compare(1, 4, 8, 0, b)

        @pl.loop(4, 8)
        def _(b):
            compare(1, 0, 8, 0, b)

    @pl.when(diagonal)
    def _():
        @pl.loop(0, 2)
        def _(p):
            @pl.loop(0, 4)
            def _(b):
                compare(p, 4, 8, p, b)

            for b in range(4, 8):
                compare(p, b, 8, p, b, True)

    def partials(act):
        for p in range(2):
            block = pick(2 * k + p, FLAT_BLOCKS)
            turn = pick(2 * k + p, BLOCK_TURN)

            def go():
                for t in range(4):
                    other = pick(4 * block + t, FLAT_SHARERS)
                    pos = pick(4 * block + t, FLAT_POS)
                    for c in range(2):
                        act(p, 2 * t + c, other, c, rbest.at[pos, mine_c, turn], recv2.at[pos, mine_c, turn], send2.at[p, t, c])

            if p:
                go()
            else:
                pl.when(diagonal)(go)

    def leave(p, a, other, c, to, rsem, ssem):
        mine = (other == k) & (mine_c == c)

        @pl.when(mine)
        def _():
            pltpu.make_async_copy(pbest.at[p, a], to, rsem).start()

        @pl.when(jnp.logical_not(mine))
        def _():
            pltpu.make_async_remote_copy(
                src_ref=pbest.at[p, a], dst_ref=to, send_sem=ssem, recv_sem=rsem,
                device_id=device_of(g, c, other), device_id_type=MESH,
            ).start()

    def left(p, a, other, c, to, rsem, ssem):
        @pl.when(jnp.logical_not((other == k) & (mine_c == c)))
        def _():
            pltpu.make_async_copy(pbest.at[p, a], pbest.at[p, a], ssem).wait()

    def condense(p):
        for a in range(8):
            pbest[p, a] = jnp.max(acc[p, a].T, axis=0, keepdims=True)

    condense(1)

    @pl.when(diagonal)
    def _():
        condense(0)

    partials(leave)

    sub = lax.broadcasted_iota(I32, (ROWS, 128), 0) & 7
    code = jnp.where(lane8 == sub8, jnp.broadcast_to(tag_in[...], (DEVS, 8, 128)), 0.0)
    code = jnp.max(code, axis=2, keepdims=True).reshape(ROWS, 1).astype(I32)
    slot_all = jnp.where(code >= 512, code - 512 + (sub >> 2) * 512, -1)

    @pl.loop(0, 16)
    def _(i):
        p, c, t = lax.div(i, 8), lax.rem(lax.div(i, 4), 2), lax.rem(i, 4)
        at = 4 * pick(2 * k + p, FLAT_BLOCKS) + t
        other = pick(at, FLAT_SHARERS)

        @pl.when((pick(at, FLAT_POS) == 1) | (other == 1) | (other == 7))
        def _():
            pltpu.make_async_copy(rbest.at[p, c, t], rbest.at[p, c, t], recv2.at[p, c, t]).wait()

    value = jnp.full((ROWS, 128), -1.0, F32)
    flipped = pick(2 * k, PHASE_POS) == 1
    for f in range(2):
        for c in range(2):
            best = jnp.where(flipped, jnp.max(rbest[1 - f, c], axis=0), jnp.max(rbest[f, c], axis=0))
            for e in range(2):
                at = lanes + (f * 512 + c * 256 + e * 128)
                value = jnp.where(slot_all == at, best[:, e * 128 : (e + 1) * 128], value)
    value = jnp.max(value, axis=1, keepdims=True)
    value = jnp.where(lanes == sub, value, -1.0).reshape(DEVS, 8, 128)
    rep[...] = jnp.max(value, axis=1, keepdims=True)

    pltpu.make_async_copy(rep.at[me], back.at[me], recv3).start()

    @pl.loop(1, DEVS)
    def _(j):
        d = lax.rem(me + 37 * j, DEVS)
        pltpu.make_async_remote_copy(
            src_ref=rep.at[d], dst_ref=back.at[me], send_sem=send3, recv_sem=recv3,
            device_id=(lax.div(d, 16), lax.rem(d, 16)), device_id_type=MESH,
        ).start()

    pltpu.make_async_copy(back, back, recv3).wait()
    mine = jnp.broadcast_to(back[...], (DEVS, 8, 128)).reshape(ROWS, 128)
    mine = jnp.max(jnp.where(lanes == sub, mine, -1.0), axis=1, keepdims=True)
    line = lax.broadcasted_iota(I32, (ROWS, 128), 0)
    for i in range(8):
        part = slice(i * 128, (i + 1) * 128)
        out_ref[:, part] = jnp.max(jnp.where(line == send_at[:, part], mine, -1.0), axis=0, keepdims=True)

    some = tag_out.at[pl.ds(0, DEVS - 1)]
    pltpu.make_async_copy(some, some, send5).wait()
    some = rep.at[pl.ds(0, DEVS - 1)]
    pltpu.make_async_copy(some, some, send3).wait()
    for f in range(2):
        some = packed.at[f, pl.ds(0, DEVS - 1)]
        pltpu.make_async_copy(some, some, send0.at[f]).wait()
        block = pick(2 * k + f, PHASE_BLOCK)
        turn = pick(2 * k + f, PHASE_TURN)
        for step in range(4):
            for flip in range(2):
                if step or flip:
                    other = pick(4 * block + lax.rem(turn + step, 4), FLAT_SHARERS)

                    @pl.when(goes(block, other, core))
                    def _():
                        pltpu.make_async_copy(split.at[0], split.at[0], send1.at[2 * f + flip, step]).wait()

        @pl.loop(0, 8)
        def _(s):
            @pl.when(passes(f, s))
            def _():
                pltpu.make_async_copy(held.at[f, s], held.at[f, s], send4.at[f, s]).wait()

    partials(left)


def on_device(embeddings, cluster, rank):
    vmem = pl.BlockSpec(memory_space=pltpu.VMEM)
    out = pl.pallas_call(
        kernel,
        out_shape=jax.ShapeDtypeStruct((1, ROWS), F32),
        in_specs=[vmem] * 3,
        out_specs=vmem,
        scratch_shapes=[
            pltpu.VMEM((ROWS, D), BF),
            pltpu.VMEM((2, DEVS, 8, PART), BF),
            pltpu.VMEM((2, DEVS, 8, PART), BF),
            pltpu.VMEM((DEVS, 1, 128), F32),
            pltpu.VMEM((DEVS, 1, 128), F32),
            pltpu.VMEM((4, HALF, D), BF),
            pltpu.VMEM((2, 8, HALF, D), BF),
            pltpu.VMEM((2, 8, HALF, 128), F32),
            pltpu.VMEM((2, 8, 1, HALF), F32),
            pltpu.VMEM((2, 2, 4, 1, HALF), F32),
            pltpu.VMEM((DEVS, 1, 128), F32),
            pltpu.VMEM((DEVS, 1, 128), F32),
            pltpu.VMEM((2, 8, 1, HALF), F32),
            pltpu.SemaphoreType.DMA((2,)),
            pltpu.SemaphoreType.DMA((2,)),
            pltpu.SemaphoreType.DMA((4, 4)),
            pltpu.SemaphoreType.DMA((2, 8)),
            pltpu.SemaphoreType.DMA((2, 4, 2)),
            pltpu.SemaphoreType.DMA((2, 2, 4)),
            pltpu.SemaphoreType.DMA,
            pltpu.SemaphoreType.DMA,
            pltpu.SemaphoreType.DMA((2, 8)),
            pltpu.SemaphoreType.DMA,
            pltpu.SemaphoreType.DMA,
        ],
        compiler_params=pltpu.CompilerParams(
            collective_id=0, has_side_effects=True, vmem_limit_bytes=56 * 2**20
        ),
        cost_estimate=pl.CostEstimate(flops=12_000_000_000, bytes_accessed=2_000_000, transcendentals=1024),
    )(embeddings, cluster.reshape(1, -1), rank.reshape(1, -1))
    return out.reshape(-1)


def solution(mesh):
    in_specs = (P(("grp", "mem"), None), P(("grp", "mem")), P(("grp", "mem")))
    out_specs = P(("grp", "mem"))
    return jax.shard_map(
        on_device, mesh=mesh, in_specs=in_specs, out_specs=out_specs, check_vma=False
    )
```

time: 121 us -> 112 us (0.926)
  Pallas kernels: 120 us -> 110 us
    pallas_call x1, Pallas kernels: 120 us -> 110 us  [on_device(): pl.pallas_call(kernel, out_shape=jax.ShapeDtypeStruct((1, ROWS), F32), in...]
where the time goes in v4:
time: 112 us
  Pallas kernels  110 us (98%)
  local copies, waits for them, and re-layouts  1.28 us (1%)
    pallas_call x1, Pallas kernels, on_device(): pl.pallas_call(kernel, out_shape=jax.ShapeDtypeStruct((1, ROWS), F32), in...  110 us

profile of v4, /device:TPU:1, one launch (start us, length us, event | category | flops | bytes accessed | tf_op | source)
XLA Modules:
  0.0 111.6 jit_solution(9714046546118740929)
XLA Ops:
  0.0 110.3 %shard_map.37 = f32[1,1024]{1,0:T(1,128)} custom-call(bf16[1024,768]{1,0:T(8,128)(2,1)} %emb_ref.1, s32[1,1024]{1,0:T(1,128)} %bitcast.4, s32[1,1024]{1,0:T(1,128)} %bitcast.5), custom_call_target="tpu_custom_call" | custom-call | flops 12000000000 | bytes 2000000 | tf_op jit(solution)/shard_map/pallas_call | solution.py:434
  110.3 1.3 %copy.5 = f32[1024]{0:T(1024)} copy(f32[1024]{0:T(1024)} %bitcast.3) | data formatting | bytes 8192

commit v5 on v4

--- a/solution.py
+++ b/solution.py
@@ -19,8 +19,16 @@
 
 BLOCKS = ((0, 1), (0, 1), (0, 2), (1, 2), (0, 3), (1, 3), (2, 3), (2, 3))
 SHARERS = ((0, 2, 1, 4), (1, 3, 0, 5), (6, 7, 2, 3), (4, 5, 6, 7))
-PLACE = ((1, 1, 0), (0, 2, 1), (2, 1, 1), (3, 1, 2), (1, 2, 0), (0, 1, 1), (2, 2, 1), (3, 2, 2))
-SPOT_OF_CLASS = (0, 6, 7, 2, 3, 1, 4, 5)
+PLACE = ((1, 3, 3), (1, 2, 2), (1, 2, 3), (0, 1, 3), (1, 3, 2), (0, 2, 2), (0, 2, 3), (0, 1, 2))
+SHIFTS = ((0, 0, 2), (1, 3, 0), (2, 2, 0))
+
+
+def chip_of(spot, g):
+    return tuple((PLACE[spot][a] + sum((g >> i & 1) * SHIFTS[i][a] for i in range(3))) % 4 for a in range(3))
+
+
+CHIPS = {chip_of(spot, g): 8 * spot + g for spot in range(8) for g in range(8)}
+WHO = [CHIPS[x, y, z] for x in range(4) for y in range(4) for z in range(4)]
 
 
 def pick(index, table):
@@ -41,10 +49,10 @@
 
 def device_of(g, c, u):
     spot = 4 * c + lax.div(u, 2)
-    turn = lax.div(g, 2)
-    x = lax.rem(pick(spot, [p[0] for p in PLACE]) + turn, 4)
-    y = lax.rem(pick(spot, [p[1] for p in PLACE]) + turn, 4)
-    z = lax.rem(pick(spot, [p[2] for p in PLACE]) + 2 * lax.rem(g, 2), 4)
+    bits = (lax.rem(g, 2), lax.rem(lax.div(g, 2), 2), lax.div(g, 4))
+    x, y, z = (
+        lax.rem(pick(spot, [p[a] for p in PLACE]) + sum(bits[i] * SHIFTS[i][a] for i in range(3)), 4) for a in range(3)
+    )
     return 2 * x + lax.rem(u, 2), 4 * z + y
 
 
@@ -52,9 +60,8 @@
     grp, mem = lax.axis_index("grp"), lax.axis_index("mem")
     x, core = lax.div(grp, 2), lax.rem(grp, 2)
     z, y = lax.div(mem, 4), lax.rem(mem, 4)
-    spot = pick(2 * lax.rem(x - y + 4, 4) + lax.rem(z, 2), SPOT_OF_CLASS)
-    turn = lax.rem(x - pick(spot, [p[0] for p in PLACE]) + 4, 4)
-    g = 2 * turn + lax.div(lax.rem(z - pick(spot, [p[2] for p in PLACE]) + 4, 4), 2)
+    who = pick(16 * x + 4 * y + z, WHO)
+    spot, g = lax.div(who, 8), lax.rem(who, 8)
     return grp, mem, g, lax.div(spot, 4), 2 * lax.rem(spot, 4) + core, core
 
 
@@ -108,9 +115,9 @@
     vk = pick_vec(share, FLAT_SHARERS)
     vp = pick_vec(share, FLAT_PHASE)
     vs = 4 * (vh & 1) + (vk >> 1)
-    vx = (pick_vec(vs, [p[0] for p in PLACE]) + (vg >> 1)) & 3
-    vy = (pick_vec(vs, [p[1] for p in PLACE]) + (vg >> 1)) & 3
-    vz = (pick_vec(vs, [p[2] for p in PLACE]) + 2 * (vg & 1)) & 3
+    vx, vy, vz = (
+        (pick_vec(vs, [p[a] for p in PLACE]) + sum((vg >> i & 1) * SHIFTS[i][a] for i in range(3))) & 3 for a in range(3)
+    )
     vdev = (2 * vx + (vk & 1)) * 16 + 4 * vz + vy
     bucket = jnp.where(alive, 2 * vdev + vp, -1)
     low = lax.broadcasted_iota(I32, (128, 256), 0)
@@ -176,6 +183,15 @@
         d = lax.rem(me + 37 * j, DEVS)
         ship(packed.at[1, d], arrived.at[1, me], d, send0.at[1], recv0.at[1])
 
+    plan = []
+    for p in range(2):
+        block = pick(2 * k + p, FLAT_BLOCKS)
+        turn = pick(2 * k + p, BLOCK_TURN)
+        for a in range(8):
+            other, c = pick(4 * block + a // 2, FLAT_SHARERS), a % 2
+            pos = pick(4 * block + a // 2, FLAT_POS)
+            plan.append((p, a, (other == k) & (mine_c == c), device_of(g, c, other), pos, turn))
+
     acc[...] = jnp.full(acc.shape, -1.0, F32)
     sub8 = lax.broadcasted_iota(I32, (DEVS, 8, 128), 1)
     lane8 = lax.broadcasted_iota(I32, (DEVS, 8, 128), 2)
@@ -215,24 +231,27 @@
         to = held.at[pick(2 * k + f, PHASE_POS), slot]
         pltpu.make_async_copy(split.at[2 * f + mine_c], to, recv1.at[pick(2 * k + f, PHASE_POS), slot]).start()
 
+        routes = []
+        for step in range(4):
+            t = lax.rem(turn + step, 4)
+            other = pick(4 * block + t, FLAT_SHARERS)
+            pos = pick(4 * block + t, FLAT_POS)
+            for flip in range(2):
+                if step or flip:
+                    c = lax.rem(mine_c + flip, 2)
+                    routes.append((step, flip, c, pos, goes(block, other, core), device_of(g, c, other)))
+
         @pl.loop(0, PIECES)
         def _(piece):
             rows = pl.ds(pl.multiple_of(piece * (HALF // PIECES), HALF // PIECES), HALF // PIECES)
-            for step in range(4):
-                t = lax.rem(turn + step, 4)
-                other = pick(4 * block + t, FLAT_SHARERS)
-                pos = pick(4 * block + t, FLAT_POS)
-                for flip in range(2):
-                    c = lax.rem(mine_c + flip, 2)
-
-                    if step or flip:
-                        @pl.when(goes(block, other, core))
-                        def _():
-                            pltpu.make_async_remote_copy(
-                                src_ref=split.at[2 * f + c, rows], dst_ref=held.at[pos, slot, rows],
-                                send_sem=send1.at[2 * f + flip, step], recv_sem=recv1.at[pos, slot],
-                                device_id=device_of(g, c, other), device_id_type=MESH,
-                            ).start()
+            for step, flip, c, pos, wanted, device in routes:
+                @pl.when(wanted)
+                def _():
+                    pltpu.make_async_remote_copy(
+                        src_ref=split.at[2 * f + c, rows], dst_ref=held.at[pos, slot, rows],
+                        send_sem=send1.at[2 * f + flip, step], recv_sem=recv1.at[pos, slot],
+                        device_id=device, device_id_type=MESH,
+                    ).start()
 
     diagonal = (k == 1) | (k == 7)
     both = (k < 2) | (k >= 6)
@@ -309,53 +328,30 @@
             for b in range(4, 8):
                 compare(p, b, 8, p, b, True)
 
-    def partials(act):
-        for p in range(2):
-            block = pick(2 * k + p, FLAT_BLOCKS)
-            turn = pick(2 * k + p, BLOCK_TURN)
-
-            def go():
-                for t in range(4):
-                    other = pick(4 * block + t, FLAT_SHARERS)
-                    pos = pick(4 * block + t, FLAT_POS)
-                    for c in range(2):
-                        act(p, 2 * t + c, other, c, rbest.at[pos, mine_c, turn], recv2.at[pos, mine_c, turn], send2.at[p, t, c])
-
-            if p:
-                go()
-            else:
-                pl.when(diagonal)(go)
-
-    def leave(p, a, other, c, to, rsem, ssem):
-        mine = (other == k) & (mine_c == c)
-
-        @pl.when(mine)
-        def _():
-            pltpu.make_async_copy(pbest.at[p, a], to, rsem).start()
-
-        @pl.when(jnp.logical_not(mine))
-        def _():
-            pltpu.make_async_remote_copy(
-                src_ref=pbest.at[p, a], dst_ref=to, send_sem=ssem, recv_sem=rsem,
-                device_id=device_of(g, c, other), device_id_type=MESH,
-            ).start()
-
-    def left(p, a, other, c, to, rsem, ssem):
-        @pl.when(jnp.logical_not((other == k) & (mine_c == c)))
-        def _():
-            pltpu.make_async_copy(pbest.at[p, a], pbest.at[p, a], ssem).wait()
-
-    def condense(p):
-        for a in range(8):
+    def leave(p):
+        for _, a, mine, device, pos, turn in plan[8 * p : 8 * p + 8]:
             pbest[p, a] = jnp.max(acc[p, a].T, axis=0, keepdims=True)
 
-    condense(1)
-
-    @pl.when(diagonal)
-    def _():
-        condense(0)
-
-    partials(leave)
+            @pl.when(mine)
+            def _():
+                to = rbest.at[pos, mine_c, turn]
+                pltpu.make_async_copy(pbest.at[p, a], to, recv2.at[pos, mine_c, turn]).start()
+
+            @pl.when(jnp.logical_not(mine))
+            def _():
+                pltpu.make_async_remote_copy(
+                    src_ref=pbest.at[p, a], dst_ref=rbest.at[pos, mine_c, turn], send_sem=send2.at[p, a // 2, a % 2],
+                    recv_sem=recv2.at[pos, mine_c, turn], device_id=device, device_id_type=MESH,
+                ).start()
+
+    def left(p):
+        for _, a, mine, device, pos, turn in plan[8 * p : 8 * p + 8]:
+            @pl.when(jnp.logical_not(mine))
+            def _():
+                pltpu.make_async_copy(pbest.at[p, a], pbest.at[p, a], send2.at[p, a // 2, a % 2]).wait()
+
+    leave(1)
+    pl.when(diagonal)(lambda: leave(0))
 
     sub = lax.broadcasted_iota(I32, (ROWS, 128), 0) & 7
     code = jnp.where(lane8 == sub8, jnp.broadcast_to(tag_in[...], (DEVS, 8, 128)), 0.0)
@@ -426,7 +422,8 @@
             def _():
                 pltpu.make_async_copy(held.at[f, s], held.at[f, s], send4.at[f, s]).wait()
 
-    partials(left)
+    left(1)
+    pl.when(diagonal)(lambda: left(0))
 
 
 def on_device(embeddings, cluster, rank):

time: 112 us -> 108 us (0.964)
  Pallas kernels: 110 us -> 106 us
    pallas_call x1, Pallas kernels: 110 us -> 106 us  [on_device(): pl.pallas_call(kernel, out_shape=jax.ShapeDtypeStruct((1, ROWS), F32), in...]
where the time goes in v5:
time: 108 us
  Pallas kernels  106 us (98%)
  local copies, waits for them, and re-layouts  1.28 us (1%)
    pallas_call x1, Pallas kernels, on_device(): pl.pallas_call(kernel, out_shape=jax.ShapeDtypeStruct((1, ROWS), F32), in...  106 us

profile of v5, /device:TPU:1, one launch (start us, length us, event | category | flops | bytes accessed | tf_op | source)
XLA Modules:
  0.0 107.7 jit_solution(4822438429282590615)
XLA Ops:
  0.0 106.4 %shard_map.37 = f32[1,1024]{1,0:T(1,128)} custom-call(bf16[1024,768]{1,0:T(8,128)(2,1)} %emb_ref.1, s32[1,1024]{1,0:T(1,128)} %bitcast.4, s32[1,1024]{1,0:T(1,128)} %bitcast.5), custom_call_target="tpu_custom_call" | custom-call | flops 12000000000 | bytes 2000000 | tf_op jit(solution)/shard_map/pallas_call | solution.py:431
  106.4 1.3 %copy.5 = f32[1024]{0:T(1024)} copy(f32[1024]{0:T(1024)} %bitcast.3) | data formatting | bytes 8192

commit v6 on v5

--- a/solution.py
+++ b/solution.py
@@ -309,22 +309,16 @@
 
     @pl.when(jnp.logical_not(diagonal))
     def _():
-        @pl.loop(0, 4)
-        def _(b):
+        for b in range(4):
             compare(1, 4, 8, 0, b)
-
-        @pl.loop(4, 8)
-        def _(b):
+        for b in range(4, 8):
             compare(1, 0, 8, 0, b)
 
     @pl.when(diagonal)
     def _():
-        @pl.loop(0, 2)
-        def _(p):
-            @pl.loop(0, 4)
-            def _(b):
+        for p in range(2):
+            for b in range(4):
                 compare(p, 4, 8, p, b)
-
             for b in range(4, 8):
                 compare(p, b, 8, p, b, True)
 

time: 108 us -> 106 us (0.981)
    pallas_call x1, Pallas kernels: 106 us -> 105 us  [on_device(): pl.pallas_call(kernel, out_shape=jax.ShapeDtypeStruct((1, ROWS), F32), in...]
where the time goes in v6:
time: 106 us
  Pallas kernels  105 us (99%)
  local copies, waits for them, and re-layouts  1.28 us (1%)
    pallas_call x1, Pallas kernels, on_device(): pl.pallas_call(kernel, out_shape=jax.ShapeDtypeStruct((1, ROWS), F32), in...  105 us

profile of v6, /device:TPU:1, one launch (start us, length us, event | category | flops | bytes accessed | tf_op | source)
XLA Modules:
  0.0 106.1 jit_solution(7959699436767434455)
XLA Ops:
  0.0 104.9 %shard_map.37 = f32[1,1024]{1,0:T(1,128)} custom-call(bf16[1024,768]{1,0:T(8,128)(2,1)} %emb_ref.1, s32[1,1024]{1,0:T(1,128)} %bitcast.4, s32[1,1024]{1,0:T(1,128)} %bitcast.5), custom_call_target="tpu_custom_call" | custom-call | flops 12000000000 | bytes 2000000 | tf_op jit(solution)/shard_map/pallas_call | solution.py:425
  104.9 1.3 %copy.5 = f32[1024]{0:T(1024)} copy(f32[1024]{0:T(1024)} %bitcast.3) | data formatting | bytes 8192

commit v7 on v6

--- a/solution.py
+++ b/solution.py
@@ -273,6 +273,7 @@
                     device_id=(grp + 1 - 2 * core, mem), device_id_type=MESH,
                 ).start()
 
+    def note(s):
         for p in range(2):
             mark = mm(probe, held[p, s], NT)[0:1, :]
             bias[p, s] = jnp.where(mark > 2.0, -1e4, 0.0)
@@ -290,6 +291,10 @@
     def _(s):
         arrive(s)
 
+    @pl.loop(0, 4)
+    def _(s):
+        note(s)
+
     @pl.when(jnp.logical_not(diagonal))
     def _():
         @pl.loop(0, 4)
@@ -306,6 +311,9 @@
     @pl.loop(4, 8)
     def _(s):
         arrive(s)
+
+    for s in range(4, 8):
+        note(s)
 
     @pl.when(jnp.logical_not(diagonal))
     def _():

time: 106 us -> 107 us (level)
  no operation moved by 1% of the time
where the time goes in v7:
time: 107 us
  Pallas kernels  106 us (99%)
  local copies, waits for them, and re-layouts  1.28 us (1%)
    pallas_call x1, Pallas kernels, on_device(): pl.pallas_call(kernel, out_shape=jax.ShapeDtypeStruct((1, ROWS), F32), in...  106 us

profile of v7, /device:TPU:1, one launch (start us, length us, event | category | flops | bytes accessed | tf_op | source)
XLA Modules:
  0.0 107.1 jit_solution(5650174017946814753)
XLA Ops:
  0.0 105.8 %shard_map.37 = f32[1,1024]{1,0:T(1,128)} custom-call(bf16[1024,768]{1,0:T(8,128)(2,1)} %emb_ref.1, s32[1,1024]{1,0:T(1,128)} %bitcast.4, s32[1,1024]{1,0:T(1,128)} %bitcast.5), custom_call_target="tpu_custom_call" | custom-call | flops 12000000000 | bytes 2000000 | tf_op jit(solution)/shard_map/pallas_call | solution.py:433
  105.8 1.3 %copy.5 = f32[1024]{0:T(1024)} copy(f32[1024]{0:T(1024)} %bitcast.3) | data formatting | bytes 8192
